TPU v7x, 512 devices: a whole 4x4x16 slice. The times are simulated.
512 devices in a mesh: seg: 32 (over z_lo, y, core), dev: 16 (over z_hi, x).
Axes of the slice: x: 4, y: 4, z: 16 (z_hi: 4, z_lo: 4; z = z_hi * 4 + z_lo), core: 2. Of those that a mesh axis runs over, the one named last changes fastest.
Arguments:
- queries: bfloat16 [65536, 1536], P(('seg', 'dev')), may hold values from -12 to 12
- keys: bfloat16 [65536, 1536], P(('seg', 'dev')), may hold values from -12 to 12
- values: bfloat16 [65536, 1536], P(('seg', 'dev')), may hold values from -4 to 4
Outputs:
- grad_queries: bfloat16 [65536, 1536], P(('seg', 'dev'))
- grad_keys: bfloat16 [65536, 1536], P(('seg', 'dev'))
- grad_values: bfloat16 [65536, 1536], P(('seg', 'dev'))
All inputs are finite; a program needn't handle non-finite values.
Results may differ from a plain program's by a relative error of at most 0.015.
Values may be sent and summed in bfloat16 or wider, within the bound.
A program may use at most 128 MiB of HBM per device.

v0:
```python
import jax
import jax.numpy as jnp
from jax import lax
from jax.sharding import PartitionSpec as P

HEADS = 16
WINDOW = 256


def passed_along(value, axis, steps):
    count = lax.axis_size(axis)
    initial, last = (max(0, -steps), min(count, count - steps))
    return lax.ppermute(value, axis, [(source, source + steps) for source in range(initial, last)])


def student_pass(block_q, ext_keys, ext_values, target, first_row, head_count):
    row_count, model_width = block_q.shape
    ext_count = ext_keys.shape[0]
    reach_rows = ext_count - row_count
    head_dim = model_width // head_count
    factor = head_dim ** (-0.5)
    query_heads = block_q.reshape(row_count, head_count, head_dim)
    key_heads = ext_keys.reshape(ext_count, head_count, head_dim)
    value_heads = ext_values.reshape(ext_count, head_count, head_dim)
    scores = (
        jnp.einsum("fhd,ehd->hfe", query_heads, key_heads, preferred_element_type=jnp.float32)
        * factor
    )
    query_pos = first_row + lax.iota(jnp.int32, row_count)
    key_pos = first_row - reach_rows + lax.iota(jnp.int32, ext_count)
    allowed = (
        (key_pos[None, :] <= query_pos[:, None])
        & (key_pos[None, :] >= query_pos[:, None] - reach_rows)
        & (key_pos[None, :] >= 0)
    )
    scores = jnp.where(allowed[None], scores, -1e30)
    row_max = scores.max(-1, keepdims=True)
    numerators = jnp.exp(scores - row_max)
    probability = numerators / numerators.sum(-1, keepdims=True)
    weights = probability.astype(jnp.bfloat16)
    output = jnp.einsum(
        "hfe,ehd->fhd", weights, value_heads, preferred_element_type=jnp.float32
    ).reshape(row_count, model_width)
    d_out = (128.0 * (output - target.astype(jnp.float32))).astype(jnp.bfloat16)
    d_out = d_out.reshape(row_count, head_count, head_dim)
    grad_v = jnp.einsum("hfe,fhd->ehd", weights, d_out, preferred_element_type=jnp.float32)
    d_prob = jnp.einsum("fhd,ehd->hfe", d_out, value_heads, preferred_element_type=jnp.float32)
    row_inner = (probability * d_prob).sum(-1, keepdims=True)
    d_scores = (probability * (d_prob - row_inner) * factor).astype(jnp.bfloat16)
    grad_q = jnp.einsum("hfe,ehd->fhd", d_scores, key_heads, preferred_element_type=jnp.float32)
    grad_k = jnp.einsum("hfe,fhd->ehd", d_scores, query_heads, preferred_element_type=jnp.float32)
    return (
        grad_q.reshape(row_count, model_width),
        grad_k.reshape(ext_count, model_width),
        grad_v.reshape(ext_count, model_width),
    )


def local(queries, keys, values):
    row_count, model_width = queries.shape
    head_count = HEADS
    head_dim = model_width // head_count
    factor = head_dim ** (-0.5)
    query_heads = queries.reshape(row_count, head_count, head_dim)
    start_state = (
        jnp.full((head_count, row_count), -1e30, jnp.float32),
        jnp.zeros((head_count, row_count), jnp.float32),
        jnp.zeros((row_count, head_count, head_dim), jnp.float32),
    )
    absorb_key_piece = lax.all_gather(keys, "dev", axis=0, tiled=True)
    absorb_value_piece = lax.all_gather(values, "dev", axis=0, tiled=True)
    piece_rows = absorb_key_piece.shape[0]
    block_rows = 256
    key_blocks = absorb_key_piece.reshape(
        piece_rows // block_rows, block_rows, head_count, head_dim
    )
    value_blocks = absorb_value_piece.reshape(
        piece_rows // block_rows, block_rows, head_count, head_dim
    )

    def one_block(block_index, inner_state):
        run_max, run_total, run_acc = inner_state
        key_block = key_blocks[block_index]
        value_block = value_blocks[block_index]
        scores = (
            jnp.einsum("fhd,khd->hfk", query_heads, key_block, preferred_element_type=jnp.float32)
            * factor
        )
        new_max = jnp.maximum(run_max, scores.max(-1))
        old_scale = jnp.exp(run_max - new_max)
        numerators = jnp.exp(scores - new_max[..., None])
        new_total = run_total * old_scale + numerators.sum(-1)
        addend = jnp.einsum(
            "hfk,khd->fhd",
            numerators.astype(jnp.bfloat16),
            value_block,
            preferred_element_type=jnp.float32,
        )
        new_acc = run_acc * jnp.transpose(old_scale)[:, :, None] + addend
        return (new_max, new_total, new_acc)

    run_max, run_total, run_acc = lax.fori_loop(0, piece_rows // block_rows, one_block, start_state)
    target = (
        (run_acc / jnp.transpose(run_total)[:, :, None])
        .reshape(row_count, model_width)
        .astype(jnp.bfloat16)
    )
    reach_count = -(-WINDOW // row_count)
    halo_keys = []
    halo_values = []
    for back_step in range(reach_count, 0, -1):
        key_piece, value_piece = passed_along((keys, values), ("seg", "dev"), back_step)
        halo_keys.append(key_piece)
        halo_values.append(value_piece)
    ext_keys = jnp.concatenate([jnp.concatenate(halo_keys, 0), keys], 0)
    ext_values = jnp.concatenate([jnp.concatenate(halo_values, 0), values], 0)
    first_row = lax.axis_index(("seg", "dev")) * row_count
    grad_q, grad_k, grad_v = student_pass(
        queries, ext_keys, ext_values, target, first_row, head_count
    )
    pad_rows = reach_count * row_count - WINDOW
    zero_rows = jnp.zeros((pad_rows, model_width), jnp.bfloat16)
    halo_grad_k = jnp.concatenate([zero_rows, grad_k[:WINDOW].astype(jnp.bfloat16)], 0)
    halo_grad_v = jnp.concatenate([zero_rows, grad_v[:WINDOW].astype(jnp.bfloat16)], 0)
    local_k = grad_k[WINDOW:]
    local_v = grad_v[WINDOW:]
    for back_step in range(reach_count, 0, -1):
        offset_rows = (reach_count - back_step) * row_count
        piece_k = halo_grad_k[offset_rows : offset_rows + row_count]
        piece_v = halo_grad_v[offset_rows : offset_rows + row_count]
        back_k, back_v = passed_along((piece_k, piece_v), ("seg", "dev"), -back_step)
        local_k = local_k + back_k.astype(jnp.float32)
        local_v = local_v + back_v.astype(jnp.float32)
    return (grad_q.astype(jnp.bfloat16), local_k.astype(jnp.bfloat16), local_v.astype(jnp.bfloat16))


def solution(mesh):
    in_specs = (P(("seg", "dev"), None), P(("seg", "dev"), None), P(("seg", "dev"), None))
    out_specs = (P(("seg", "dev"), None), P(("seg", "dev"), None), P(("seg", "dev"), None))
    return jax.shard_map(local, mesh=mesh, in_specs=in_specs, out_specs=out_specs, check_vma=False)
```

profile of v0, /device:TPU:36, one launch (start us, length us, event | category | flops | bytes accessed | tf_op | source)
XLA Modules:
  0.0 665.9 jit_solution(2360740809766414248)
XLA Ops:
  8.6 3.1 collective-permute-start.1
  11.8 9.3 %collective-permute-start = (bf16[128,1536]{1,0:T(8,128)(2,1)}, bf16[128,1536]{1,0:T(8,128)(2,1)}, u32[]{:S(2)}, u32[]{:S(2)}) collective-permute-start(bf16[128,1536]{1,0:T(8,128)(2,1)} %param.6), channel_id=1, source_target_pairs={{0,2},{1,3},{2,4},{3,5},{4,6},{5,7},{6,8},{7,9},{8,10},{9,11},{10,... | collective-permute-start | bytes 1179656 | tf_op jit(solution)/shard_map/ppermute | solution.py:13
  21.1 4.0 collective-permute-start.3
  25.1 8.1 %collective-permute-start.2 = (bf16[128,1536]{1,0:T(8,128)(2,1)}, bf16[128,1536]{1,0:T(8,128)(2,1)}, u32[]{:S(2)}, u32[]{:S(2)}) collective-permute-start(bf16[128,1536]{1,0:T(8,128)(2,1)} %param.7), channel_id=1, source_target_pairs={{0,2},{1,3},{2,4},{3,5},{4,6},{5,7},{6,8},{7,9},{8,10},{9,11},{10,... | collective-permute-start | bytes 1179656 | tf_op jit(solution)/shard_map/ppermute | solution.py:13
  35.6 43.7 %collective-permute-done = bf16[128,1536]{1,0:T(8,128)(2,1)} collective-permute-done((bf16[128,1536]{1,0:T(8,128)(2,1)}, bf16[128,1536]{1,0:T(8,128)(2,1)}, u32[]{:S(2)}, u32[]{:S(2)}) %collective-permute-start) | collective-permute-done | bytes 393248 | tf_op jit(solution)/shard_map/ppermute | solution.py:13
  82.1 11.5 %collective-permute-done.2 = bf16[128,1536]{1,0:T(8,128)(2,1)} collective-permute-done((bf16[128,1536]{1,0:T(8,128)(2,1)}, bf16[128,1536]{1,0:T(8,128)(2,1)}, u32[]{:S(2)}, u32[]{:S(2)}) %collective-permute-start.2) | collective-permute-done | bytes 393248 | tf_op jit(solution)/shard_map/ppermute | solution.py:13
  96.1 4.2 fusion.55
  100.3 183.1 %all-gather.3.cloned.1.call-done = bf16[2048,1536]{1,0:T(8,128)(2,1)} async-done(((bf16[128,1536]{1,0:T(8,128)(2,1)}), bf16[2048,1536]{1,0:T(8,128)(2,1)}) %all-gather.3.cloned.1.call-update) | async-done | bytes 6291472 | tf_op jit(solution)/shard_map/all_gather | solution.py:70
  283.4 13.7 %reshape.136 = bf16[8,256,16,96]{3,2,1,0:T(8,128)(2,1)} reshape(bf16[2048,1536]{1,0:T(8,128)(2,1)} %all-gather.3.cloned.1.call-done) | data formatting | bytes 12582912 | tf_op jit(solution)/shard_map/reshape | solution.py:74
  297.1 11.8 %copy.30 = bf16[8,256,16,96]{1,3,2,0:T(8,128)(2,1)} copy(bf16[8,256,16,96]{3,2,1,0:T(8,128)(2,1)} %reshape.136) | data formatting | bytes 12582912
  308.8 111.1 %all-gather.5.cloned.1.call-done = bf16[2048,1536]{1,0:T(8,128)(2,1)} async-done(((bf16[128,1536]{1,0:T(8,128)(2,1)}), bf16[2048,1536]{1,0:T(8,128)(2,1)}) %all-gather.5.cloned.1.call-update) | async-done | bytes 6291472 | tf_op jit(solution)/shard_map/all_gather | solution.py:71
  419.9 13.7 %reshape.137 = bf16[8,256,16,96]{3,2,1,0:T(8,128)(2,1)} reshape(bf16[2048,1536]{1,0:T(8,128)(2,1)} %all-gather.5.cloned.1.call-done) | data formatting | bytes 12582912 | tf_op jit(solution)/shard_map/reshape | solution.py:77
  433.6 11.7 %copy.31 = bf16[8,256,16,96]{1,3,2,0:T(8,128)(2,1)} copy(bf16[8,256,16,96]{3,2,1,0:T(8,128)(2,1)} %reshape.137) | data formatting | bytes 12582912
  445.2 31.1 %while.18 = (s32[]{:T(128)}, f32[16,128]{1,0:T(8,128)S(1)}, f32[16,128]{1,0:T(8,128)S(1)}, f32[128,16,96]{0,2,1:T(8,128)S(1)}, bf16[8,256,16,96]{1,3,2,0:T(8,128...) while((s32[]{:T(128)}, f32[16,128]{1,0:T(8,128)S(1)}, ...), condition=%wide.region_5.6_spmd.clone, body=%wide.region_2.5_spmd.clone.sunk | while | flops 206123008 | bytes 9961593 | solution.py:102
  476.4 2.8 fusion.39
  479.2 2.3 fusion.60
  481.8 2.8 fusion.59
  484.6 7.6 %fusion.56 = (bf16[384,16,96]{0,2,1:T(8,128)(2,1)}, f32[384,16,96]{0,2,1:T(8,128)}) fusion(bf16[128,16,96]{0,2,1:T(8,128)(2,1)S(1)} %get-tuple-element.277, f32[16,128,384]{1,2,0:T(8,128)} %fusion.60, f32[16,128,384]{1,2,0:T(8,128)} %get-tuple-element.190, f32[16,128]{1,0:T(8,128)S(1)} %get-tuple-element.189), kind=kOutput, calls=%fused_computation.68 | convolution fusion | flops 157092224 | bytes 10231808 | tf_op jit(solution)/shard_map/hfe,fhd->ehd/dot_general | solution.py:51
  493.7 2.5 collective-permute-start.5
  496.4 52.0 %collective-permute-start.4 = (bf16[128,1536]{1,0:T(8,128)(2,1)S(1)}, bf16[128,1536]{1,0:T(8,128)(2,1)}, u32[]{:S(2)}, u32[]{:S(2)}) collective-permute-start(bf16[128,1536]{1,0:T(8,128)(2,1)S(1)} %copy.36), channel_id=1, source_target_pairs={{2,0},{3,1},{4,2},{5,3},{6,4},{7,5},{8,6},{9,7},{10,8},{11,9},{12,... | collective-permute-start | bytes 1179656 | tf_op jit(solution)/shard_map/ppermute | solution.py:13
  548.3 5.9 fusion.40
  562.3 3.4 collective-permute-start.6
  565.7 2.0 add_convert_fusion.1
  568.7 88.5 %collective-permute-done.6 = bf16[128,1536]{1,0:T(8,128)(2,1)S(1)} collective-permute-done((bf16[128,1536]{1,0:T(8,128)(2,1)S(1)}, bf16[128,1536]{1,0:T(8,128)(2,1)S(1)}, u32[]{:S(2)}, u32[]{:S(2)}) %collective-permute-start.6) | collective-permute-done | bytes 393248 | tf_op jit(solution)/shard_map/ppermute | solution.py:13
  (92 shorter events, 52.6 us)
Async XLA Ops:
  7.2 276.2 %all-gather.3.cloned.1.call-start = ((), (), s32[]{:S(2)}) async-start(), calls=%async_computation | async-start | bytes 6684672 | tf_op jit(solution)/shard_map/all_gather | solution.py:70
  7.9 412.0 %all-gather.5.cloned.1.call-start = ((), (), s32[]{:S(2)}) async-start(), calls=%async_computation.1 | async-start | bytes 6684672 | tf_op jit(solution)/shard_map/all_gather | solution.py:71
  8.6 26.2 %collective-permute-start.1 = (bf16[128,1536]{1,0:T(8,128)(2,1)}, bf16[128,1536]{1,0:T(8,128)(2,1)S(1)}, u32[]{:S(2)}, u32[]{:S(2)}) collective-permute-start(bf16[128,1536]{1,0:T(8,128)(2,1)} %param.6), channel_id=1, source_target_pairs={{0,1},{1,2},{2,3},{3,4},{4,5},{5,6},{6,7},{7,8},{8,9},{9,10},{10,1... | collective-permute-start | bytes 1179656 | tf_op jit(solution)/shard_map/ppermute | solution.py:13
  11.8 67.6 %collective-permute-start = (bf16[128,1536]{1,0:T(8,128)(2,1)}, bf16[128,1536]{1,0:T(8,128)(2,1)}, u32[]{:S(2)}, u32[]{:S(2)}) collective-permute-start(bf16[128,1536]{1,0:T(8,128)(2,1)} %param.6), channel_id=1, source_target_pairs={{0,2},{1,3},{2,4},{3,5},{4,6},{5,7},{6,8},{7,9},{8,10},{9,11},{10,... | collective-permute-start | bytes 1179656 | tf_op jit(solution)/shard_map/ppermute | solution.py:13
  21.1 61.0 %collective-permute-start.3 = (bf16[128,1536]{1,0:T(8,128)(2,1)}, bf16[128,1536]{1,0:T(8,128)(2,1)S(1)}, u32[]{:S(2)}, u32[]{:S(2)}) collective-permute-start(bf16[128,1536]{1,0:T(8,128)(2,1)} %param.7), channel_id=1, source_target_pairs={{0,1},{1,2},{2,3},{3,4},{4,5},{5,6},{6,7},{7,8},{8,9},{9,10},{10,1... | collective-permute-start | bytes 1179656 | tf_op jit(solution)/shard_map/ppermute | solution.py:13
  25.1 68.5 %collective-permute-start.2 = (bf16[128,1536]{1,0:T(8,128)(2,1)}, bf16[128,1536]{1,0:T(8,128)(2,1)}, u32[]{:S(2)}, u32[]{:S(2)}) collective-permute-start(bf16[128,1536]{1,0:T(8,128)(2,1)} %param.7), channel_id=1, source_target_pairs={{0,2},{1,3},{2,4},{3,5},{4,6},{5,7},{6,8},{7,9},{8,10},{9,11},{10,... | collective-permute-start | bytes 1179656 | tf_op jit(solution)/shard_map/ppermute | solution.py:13
  34.8 58.8 %copy-start.1 = (bf16[128,1536]{1,0:T(8,128)(2,1)S(1)}, bf16[128,1536]{1,0:T(8,128)(2,1)}, u32[]{:S(2)}) copy-start(bf16[128,1536]{1,0:T(8,128)(2,1)} %param.7) | copy-start | bytes 1179652
  34.8 0.7 copy-start.3
  476.4 2.9 copy-start
  479.2 2.6 copy-start.4
  492.3 56.1 %copy-start.2 = (bf16[384,1536]{0,1:T(8,128)(2,1)S(1)}, bf16[384,1536]{0,1:T(8,128)(2,1)}, u32[]{:S(2)}) copy-start(bf16[384,1536]{0,1:T(8,128)(2,1)} %copy.24) | copy-start | bytes 3538948
  493.7 72.0 %collective-permute-start.5 = (bf16[128,1536]{1,0:T(8,128)(2,1)S(1)}, bf16[128,1536]{1,0:T(8,128)(2,1)}, u32[]{:S(2)}, u32[]{:S(2)}) collective-permute-start(bf16[128,1536]{1,0:T(8,128)(2,1)S(1)} %copy.38), channel_id=1, source_target_pairs={{1,0},{2,1},{3,2},{4,3},{5,4},{6,5},{7,6},{8,7},{9,8},{10,9},{11,1... | collective-permute-start | bytes 1179656 | tf_op jit(solution)/shard_map/ppermute | solution.py:13
  496.4 69.3 %collective-permute-start.4 = (bf16[128,1536]{1,0:T(8,128)(2,1)S(1)}, bf16[128,1536]{1,0:T(8,128)(2,1)}, u32[]{:S(2)}, u32[]{:S(2)}) collective-permute-start(bf16[128,1536]{1,0:T(8,128)(2,1)S(1)} %copy.36), channel_id=1, source_target_pairs={{2,0},{3,1},{4,2},{5,3},{6,4},{7,5},{8,6},{9,7},{10,8},{11,9},{12,... | collective-permute-start | bytes 1179656 | tf_op jit(solution)/shard_map/ppermute | solution.py:13
  558.7 10.0 %collective-permute-start.7 = (bf16[128,1536]{1,0:T(8,128)(2,1)}, bf16[128,1536]{1,0:T(8,128)(2,1)}, u32[]{:S(2)}, u32[]{:S(2)}) collective-permute-start(bf16[128,1536]{1,0:T(8,128)(2,1)} %copy.42), channel_id=1, source_target_pairs={{1,0},{2,1},{3,2},{4,3},{5,4},{6,5},{7,6},{8,7},{9,8},{10,9},{11,1... | collective-permute-start | bytes 1179656 | tf_op jit(solution)/shard_map/ppermute | solution.py:13
  562.3 94.9 %collective-permute-start.6 = (bf16[128,1536]{1,0:T(8,128)(2,1)S(1)}, bf16[128,1536]{1,0:T(8,128)(2,1)S(1)}, u32[]{:S(2)}, u32[]{:S(2)}) collective-permute-start(bf16[128,1536]{1,0:T(8,128)(2,1)S(1)} %copy.40), channel_id=1, source_target_pairs={{2,0},{3,1},{4,2},{5,3},{6,4},{7,5},{8,6},{9,7},{10,8},{11,9},{12,... | collective-permute-start | bytes 1179656 | tf_op jit(solution)/shard_map/ppermute | solution.py:13
Sparse Core Ops, SparseCore 0:
  11.0 272.3 all-gather.2
  286.4 133.4 all-gather.4
where the time goes:
time: 668 us; the launch traced here: 666 us
  waiting for transfers between devices  440 us (66%)
  starting transfers between devices  84.4 us (13%)
  local copies, waits for them, and re-layouts  63.8 us (10%)
  matrix products  53.1 us (8%)
  between operations  14.3 us (2%)
  other arithmetic  9.59 us (1%)
    all_gather x1, waiting for transfers between devices, local(): absorb_key_piece = lax.all_gather(keys, 'dev', axis=0, tiled=True)  183 us
    ppermute x8, waiting for transfers between devices, passed_along(): lax.ppermute(value, axis, [(source, source + steps) for source in range(i...  145 us
    all_gather x1, waiting for transfers between devices, local(): absorb_value_piece = lax.all_gather(values, 'dev', axis=0, tiled=True)  111 us
    ppermute x8, starting transfers between devices, passed_along(): lax.ppermute(value, axis, [(source, source + steps) for source in range(i...  84.3 us
    unnamed x14, local copies, waits for them, and re-layouts  26.7 us
    dot_general x8, matrix products, one_block(): jnp.einsum('hfk,khd->fhd', numerators.astype(jnp.bfloat16), value_block,...  14.5 us
    reshape x1, local copies, waits for them, and re-layouts, local(): absorb_key_piece.reshape(piece_rows // block_rows, block_rows, head_count...  13.7 us
    reshape x1, local copies, waits for them, and re-layouts, local(): absorb_value_piece.reshape(piece_rows // block_rows, block_rows, head_cou...  13.7 us
  transfers between devices with their start and end apart: 10, of which 6 were waited for; matrix products, arithmetic and copies ran while one was open for 8% of the time, Pallas kernels for 0%

commit v1 on v0

--- a/solution.py
+++ b/solution.py
@@ -68,7 +68,15 @@
         jnp.zeros((row_count, head_count, head_dim), jnp.float32),
     )
     absorb_key_piece = lax.all_gather(keys, "dev", axis=0, tiled=True)
-    absorb_value_piece = lax.all_gather(values, "dev", axis=0, tiled=True)
+    absorb_value_piece = jnp.concatenate(
+        lax.all_to_all(
+            jnp.stack([values for _ in range(lax.axis_size("dev"))], 0),
+            "dev",
+            split_axis=0,
+            concat_axis=0,
+        ),
+        0,
+    )
     piece_rows = absorb_key_piece.shape[0]
     block_rows = 256
     key_blocks = absorb_key_piece.reshape(

time: 668 us -> 819 us (1.23)
  the two profiles are of different devices: /device:TPU:36 before, /device:TPU:269 now
where the time goes in v1:
time: 819 us; the launch traced here: 817 us
  waiting for transfers between devices  619 us (76%)
  local copies, waits for them, and re-layouts  67.7 us (8%)
  matrix products  53.7 us (7%)
  starting transfers between devices  52.4 us (6%)
  between operations  14.3 us (2%)
  other arithmetic  9.59 us (1%)
    ppermute x8, waiting for transfers between devices, passed_along(): lax.ppermute(value, axis, [(source, source + steps) for source in range(i...  345 us
    all_gather x1, waiting for transfers between devices, local(): absorb_key_piece = lax.all_gather(keys, 'dev', axis=0, tiled=True)  274 us
    ppermute x8, starting transfers between devices, passed_along(): lax.ppermute(value, axis, [(source, source + steps) for source in range(i...  38.3 us
    unnamed x19, local copies, waits for them, and re-layouts  22.1 us
  transfers between devices with their start and end apart: 10, of which 7 were waited for; matrix products, arithmetic and copies ran while one was open for 6% of the time, Pallas kernels for 0%

profile of v1, /device:TPU:269, one launch (start us, length us, event | category | flops | bytes accessed | tf_op | source)
XLA Modules:
  0.0 817.1 jit_solution(18053480699231254651)
XLA Ops:
  8.4 3.8 stack.2
  12.2 14.0 %all-to-all-start = ((bf16[16,128,1536]{1,2,0:T(8,128)(2,1)}), bf16[16,128,1536]{1,2,0:T(8,128)(2,1)}, u32[]{:S(2)}, u32[]{:S(2)}) async-start(bf16[16,128,1536]{1,2,0:T(8,128)(2,1)} %stack.2), calls=%async_computation | async-start | bytes 12582912 | tf_op jit(solution)/shard_map/all_to_all | solution.py:72
  26.9 2.8 collective-permute-start.1
  32.2 3.7 collective-permute-start.3
  36.0 3.9 collective-permute-start.2
  40.4 23.0 %collective-permute-done.1 = bf16[128,1536]{1,0:T(8,128)(2,1)S(1)} collective-permute-done((bf16[128,1536]{1,0:T(8,128)(2,1)S(1)}, bf16[128,1536]{1,0:T(8,128)(2,1)S(1)}, u32[]{:S(2)}, u32[]{:S(2)}) %collective-permute-start.1) | collective-permute-done | bytes 393248 | tf_op jit(solution)/shard_map/ppermute | solution.py:13
  64.1 137.6 %collective-permute-done = bf16[128,1536]{1,0:T(8,128)(2,1)} collective-permute-done((bf16[128,1536]{1,0:T(8,128)(2,1)S(1)}, bf16[128,1536]{1,0:T(8,128)(2,1)}, u32[]{:S(2)}, u32[]{:S(2)}) %collective-permute-start) | collective-permute-done | bytes 393248 | tf_op jit(solution)/shard_map/ppermute | solution.py:13
  204.3 16.5 %collective-permute-done.2 = bf16[128,1536]{1,0:T(8,128)(2,1)} collective-permute-done((bf16[128,1536]{1,0:T(8,128)(2,1)S(1)}, bf16[128,1536]{1,0:T(8,128)(2,1)}, u32[]{:S(2)}, u32[]{:S(2)}) %collective-permute-start.2) | collective-permute-done | bytes 393248 | tf_op jit(solution)/shard_map/ppermute | solution.py:13
  223.5 4.3 fusion.55
  227.8 273.6 %all-gather.2.cloned.1.call-done = bf16[2048,1536]{1,0:T(8,128)(2,1)} async-done(((bf16[128,1536]{1,0:T(8,128)(2,1)}), bf16[2048,1536]{1,0:T(8,128)(2,1)}) %all-gather.2.cloned.1.call-update) | async-done | bytes 6291472 | tf_op jit(solution)/shard_map/all_gather | solution.py:70
  501.4 13.7 %reshape.134 = bf16[8,256,16,96]{3,2,1,0:T(8,128)(2,1)} reshape(bf16[2048,1536]{1,0:T(8,128)(2,1)} %all-gather.2.cloned.1.call-done) | data formatting | bytes 12582912 | tf_op jit(solution)/shard_map/reshape | solution.py:82
  515.0 11.7 %copy.52 = bf16[8,256,16,96]{1,3,2,0:T(8,128)(2,1)} copy(bf16[8,256,16,96]{3,2,1,0:T(8,128)(2,1)} %reshape.134) | data formatting | bytes 12582912
  526.8 8.5 %copy.51 = bf16[16,128,1536]{1,0,2:T(8,128)(2,1)} copy(bf16[16,128,1536]{1,2,0:T(8,128)(2,1)} %all-to-all-done) | data formatting | bytes 12582912 | tf_op jit(solution)/shard_map/all_to_all | solution.py:72
  535.3 10.0 %reshape_reshape.3 = bf16[8,256,16,96]{1,0,3,2:T(8,128)(2,1)} reshape(bf16[16,128,1536]{1,0,2:T(8,128)(2,1)} %copy.51) | data formatting | bytes 12582912 | tf_op jit(solution)/shard_map/reshape;reshape | solution.py:85
  545.3 7.0 copy.53
  552.2 31.1 %while.18 = (s32[]{:T(128)}, f32[16,128]{1,0:T(8,128)S(1)}, f32[16,128]{1,0:T(8,128)S(1)}, f32[128,16,96]{0,2,1:T(8,128)S(1)}, bf16[8,256,16,96]{1,3,2,0:T(8,128...) while((s32[]{:T(128)}, f32[16,128]{1,0:T(8,128)S(1)}, ...), condition=%wide.region_5.6_spmd.clone, body=%wide.region_2.5_spmd.clone.sunk | while | flops 206123008 | bytes 9961593 | solution.py:110
  583.4 2.8 fusion.39
  588.8 2.8 fusion.59
  591.6 7.9 fusion.56
  603.0 19.7 %collective-permute-start.4 = (bf16[128,1536]{1,0:T(8,128)(2,1)S(1)}, bf16[128,1536]{1,0:T(8,128)(2,1)}, u32[]{:S(2)}, u32[]{:S(2)}) collective-permute-start(bf16[128,1536]{1,0:T(8,128)(2,1)S(1)} %copy.58), channel_id=1, source_target_pairs={{2,0},{3,1},{4,2},{5,3},{6,4},{7,5},{8,6},{9,7},{10,8},{11,9},{12,... | collective-permute-start | bytes 1179656 | tf_op jit(solution)/shard_map/ppermute | solution.py:13
  622.8 6.1 fusion.40
  638.9 41.6 %collective-permute-done.5 = bf16[128,1536]{1,0:T(8,128)(2,1)} collective-permute-done((bf16[128,1536]{1,0:T(8,128)(2,1)S(1)}, bf16[128,1536]{1,0:T(8,128)(2,1)}, u32[]{:S(2)}, u32[]{:S(2)}) %collective-permute-start.5) | collective-permute-done | bytes 393248 | tf_op jit(solution)/shard_map/ppermute | solution.py:13
  680.5 111.1 %collective-permute-done.4 = bf16[128,1536]{1,0:T(8,128)(2,1)} collective-permute-done((bf16[128,1536]{1,0:T(8,128)(2,1)S(1)}, bf16[128,1536]{1,0:T(8,128)(2,1)}, u32[]{:S(2)}, u32[]{:S(2)}) %collective-permute-start.4) | collective-permute-done | bytes 393248 | tf_op jit(solution)/shard_map/ppermute | solution.py:13
  793.6 14.8 %collective-permute-done.6 = bf16[128,1536]{1,0:T(8,128)(2,1)S(1)} collective-permute-done((bf16[128,1536]{1,0:T(8,128)(2,1)S(1)}, bf16[128,1536]{1,0:T(8,128)(2,1)S(1)}, u32[]{:S(2)}, u32[]{:S(2)}) %collective-permute-start.6) | collective-permute-done | bytes 393248 | tf_op jit(solution)/shard_map/ppermute | solution.py:13
  (98 shorter events, 61.4 us)
Async XLA Ops:
  12.2 14.7 %copy-start.2 = (bf16[128,1536]{1,0:T(8,128)(2,1)S(1)}, bf16[128,1536]{1,0:T(8,128)(2,1)}, u32[]{:S(2)}) copy-start(bf16[128,1536]{1,0:T(8,128)(2,1)} %param.6) | copy-start | bytes 1179652
  12.2 20.1 %copy-start.1 = (bf16[128,1536]{1,0:T(8,128)(2,1)S(1)}, bf16[128,1536]{1,0:T(8,128)(2,1)}, u32[]{:S(2)}) copy-start(bf16[128,1536]{1,0:T(8,128)(2,1)} %param.7) | copy-start | bytes 1179652
  12.2 27.7 %copy-start.5 = (bf16[128,1536]{1,0:T(8,128)(2,1)S(1)}, bf16[128,1536]{1,0:T(8,128)(2,1)}, u32[]{:S(2)}) copy-start(bf16[128,1536]{1,0:T(8,128)(2,1)} %param.5) | copy-start | bytes 1179652
  12.2 514.6 %all-to-all-start = ((bf16[16,128,1536]{1,2,0:T(8,128)(2,1)}), bf16[16,128,1536]{1,2,0:T(8,128)(2,1)}, u32[]{:S(2)}, u32[]{:S(2)}) async-start(bf16[16,128,1536]{1,2,0:T(8,128)(2,1)} %stack.2), calls=%async_computation | async-start | bytes 12582912 | tf_op jit(solution)/shard_map/all_to_all | solution.py:72
  26.2 475.2 %all-gather.2.cloned.1.call-start = ((), (), s32[]{:S(2)}) async-start(), calls=%async_computation.1 | async-start | bytes 6684672 | tf_op jit(solution)/shard_map/all_gather | solution.py:70
  26.9 36.4 %collective-permute-start.1 = (bf16[128,1536]{1,0:T(8,128)(2,1)S(1)}, bf16[128,1536]{1,0:T(8,128)(2,1)S(1)}, u32[]{:S(2)}, u32[]{:S(2)}) collective-permute-start(bf16[128,1536]{1,0:T(8,128)(2,1)S(1)} %copy-done.2), channel_id=1, source_target_pairs={{0,1},{1,2},{2,3},{3,4},{4,5},{5,6},{6,7},{7,8},{8,9},{9,10},{10,1... | collective-permute-start | bytes 1179656 | tf_op jit(solution)/shard_map/ppermute | solution.py:13
  29.7 172.0 %collective-permute-start = (bf16[128,1536]{1,0:T(8,128)(2,1)S(1)}, bf16[128,1536]{1,0:T(8,128)(2,1)}, u32[]{:S(2)}, u32[]{:S(2)}) collective-permute-start(bf16[128,1536]{1,0:T(8,128)(2,1)S(1)} %copy-done.2), channel_id=1, source_target_pairs={{0,2},{1,3},{2,4},{3,5},{4,6},{5,7},{6,8},{7,9},{8,10},{9,11},{10,... | collective-permute-start | bytes 1179656 | tf_op jit(solution)/shard_map/ppermute | solution.py:13
  32.2 172.1 %collective-permute-start.3 = (bf16[128,1536]{1,0:T(8,128)(2,1)S(1)}, bf16[128,1536]{1,0:T(8,128)(2,1)}, u32[]{:S(2)}, u32[]{:S(2)}) collective-permute-start(bf16[128,1536]{1,0:T(8,128)(2,1)S(1)} %copy-done.1), channel_id=1, source_target_pairs={{0,1},{1,2},{2,3},{3,4},{4,5},{5,6},{6,7},{7,8},{8,9},{9,10},{10,1... | collective-permute-start | bytes 1179656 | tf_op jit(solution)/shard_map/ppermute | solution.py:13
  36.0 184.9 %collective-permute-start.2 = (bf16[128,1536]{1,0:T(8,128)(2,1)S(1)}, bf16[128,1536]{1,0:T(8,128)(2,1)}, u32[]{:S(2)}, u32[]{:S(2)}) collective-permute-start(bf16[128,1536]{1,0:T(8,128)(2,1)S(1)} %copy-done.1), channel_id=1, source_target_pairs={{0,2},{1,3},{2,4},{3,5},{4,6},{5,7},{6,8},{7,9},{8,10},{9,11},{10,... | collective-permute-start | bytes 1179656 | tf_op jit(solution)/shard_map/ppermute | solution.py:13
  63.3 0.7 copy-start.4
  583.4 2.9 copy-start
  586.2 2.6 copy-start.6
  599.5 23.3 %copy-start.3 = (bf16[384,1536]{0,1:T(8,128)(2,1)S(1)}, bf16[384,1536]{0,1:T(8,128)(2,1)}, u32[]{:S(2)}) copy-start(bf16[384,1536]{0,1:T(8,128)(2,1)} %copy.45) | copy-start | bytes 3538948
  600.9 79.6 %collective-permute-start.5 = (bf16[128,1536]{1,0:T(8,128)(2,1)S(1)}, bf16[128,1536]{1,0:T(8,128)(2,1)}, u32[]{:S(2)}, u32[]{:S(2)}) collective-permute-start(bf16[128,1536]{1,0:T(8,128)(2,1)S(1)} %copy.60), channel_id=1, source_target_pairs={{1,0},{2,1},{3,2},{4,3},{5,4},{6,5},{7,6},{8,7},{9,8},{10,9},{11,1... | collective-permute-start | bytes 1179656 | tf_op jit(solution)/shard_map/ppermute | solution.py:13
  603.0 188.6 %collective-permute-start.4 = (bf16[128,1536]{1,0:T(8,128)(2,1)S(1)}, bf16[128,1536]{1,0:T(8,128)(2,1)}, u32[]{:S(2)}, u32[]{:S(2)}) collective-permute-start(bf16[128,1536]{1,0:T(8,128)(2,1)S(1)} %copy.58), channel_id=1, source_target_pairs={{2,0},{3,1},{4,2},{5,3},{6,4},{7,5},{8,6},{9,7},{10,8},{11,9},{12,... | collective-permute-start | bytes 1179656 | tf_op jit(solution)/shard_map/ppermute | solution.py:13
  633.4 160.2 %collective-permute-start.7 = (bf16[128,1536]{1,0:T(8,128)(2,1)}, bf16[128,1536]{1,0:T(8,128)(2,1)}, u32[]{:S(2)}, u32[]{:S(2)}) collective-permute-start(bf16[128,1536]{1,0:T(8,128)(2,1)} %copy.64), channel_id=1, source_target_pairs={{1,0},{2,1},{3,2},{4,3},{5,4},{6,5},{7,6},{8,7},{9,8},{10,9},{11,1... | collective-permute-start | bytes 1179656 | tf_op jit(solution)/shard_map/ppermute | solution.py:13
  637.0 171.4 %collective-permute-start.6 = (bf16[128,1536]{1,0:T(8,128)(2,1)S(1)}, bf16[128,1536]{1,0:T(8,128)(2,1)S(1)}, u32[]{:S(2)}, u32[]{:S(2)}) collective-permute-start(bf16[128,1536]{1,0:T(8,128)(2,1)S(1)} %copy.62), channel_id=1, source_target_pairs={{2,0},{3,1},{4,2},{5,3},{6,4},{7,5},{8,6},{9,7},{10,8},{11,9},{12,... | collective-permute-start | bytes 1179656 | tf_op jit(solution)/shard_map/ppermute | solution.py:13
Sparse Core Ops, SparseCore 0:
  30.0 471.2 all-gather.1
